TPU v7x, 512 devices: a whole 4x8x8 slice. The times are simulated.
512 devices in a mesh: batch: 2 (over core), token: 32 (over x, z), hidden: 8 (over y).
Axes of the slice: x: 4, y: 8, z: 8, core: 2. Of those that a mesh axis runs over, the one named last changes fastest.
Arguments:
- hist_len: int32 [512], replicated, may hold values from 32 to 512, as said below
- queries: bfloat16 [32, 1536], P(None, 'token'), may hold values from -4 to 4
- history_keys: bfloat16 [1536, 1536, 128], P(('batch', 'hidden'), 'token'), may hold values from -192 to 192
- cached_history_values: bfloat16 [1536, 1536, 128], P(('batch', 'hidden'), 'token'), may hold values from -6 to 6
- gain_mix: float32 [1536], replicated, may hold values from 0.25 to 1.75
- w_up: bfloat16 [32, 1536, 3072], P('token', None, 'hidden'), may hold values from -0.15625 to 0.15625
- w_down: bfloat16 [32, 3072, 1536], P('token', 'hidden'), may hold values from -0.109375 to 0.109375
- gain_out: float32 [1536], replicated, may hold values from 0.25 to 1.75
Outputs:
- mixer_out: bfloat16 [512, 32, 1536], P(('batch', 'hidden'), 'token')
Inputs may be any that keep to these rules, and one draw needn't show every extreme that they name: `hist_len`: along batch+hidden, the requests of each index need between 32 and 96 slots, indices 2i and 2i + 1 need 4 * 32 slots together, and some index needs exactly 96; within an index, requests 2j and 2j + 1 need from 2 to 6 slots together.
All inputs are finite; a program needn't handle non-finite values.
Results may differ from a plain program's by a relative error of at most 0.015.
Values may be sent and summed in bfloat16 or wider, within the bound.
A program may use at most 64 MiB of HBM per device.

v0:
```python
import jax
import jax.numpy as jnp
from jax import lax
from jax.sharding import PartitionSpec as P

TOKEN_COUNT = 32
MODEL_WIDTH = 1536
BLOCK_POSITIONS = 128
REQ_DEV = 32
EPSILON = 1e-05
NEGATIVE_FILL = -1e30


def in_blocks(x, dim, length):
    dims = x.shape
    parts = x.reshape(*dims[:dim], length, dims[dim] // length, *dims[dim + 1 :])
    return jnp.moveaxis(parts, dim, 0)


def sent_and_summed(x, axis, dim):
    length = lax.axis_size(axis)
    parts = lax.all_to_all(in_blocks(x, dim, length), axis, 0, 0, tiled=True)
    return jnp.sum(parts.astype(jnp.float32), axis=0)


def slot_layout(lengths, slot_count, block_rows):
    request_count = lengths.shape[0]
    blocks = (lengths + block_rows - 1) // block_rows
    block_ends = jnp.cumsum(blocks)
    block_starts = block_ends - blocks
    slot_index = jnp.arange(slot_count, dtype=jnp.int32)
    owners = jnp.sum((block_ends[None, :] <= slot_index[:, None]).astype(jnp.int32), axis=1)
    onehot = owners[:, None] == jnp.arange(request_count, dtype=jnp.int32)[None, :]
    start_of = jnp.sum(jnp.where(onehot, block_starts[None, :], 0), axis=1)
    length_of = jnp.sum(jnp.where(onehot, lengths[None, :], 0), axis=1)
    valid_rows = jnp.clip(length_of - (slot_index - start_of) * block_rows, 0, block_rows)
    return (onehot, valid_rows)


def block_partials(query_heads, slot_keys, slot_values, valid_rows, score_scale):
    scores = (
        jnp.einsum("qhs,nhsp->nqhp", query_heads, slot_keys, preferred_element_type=jnp.float32)
        * score_scale
    )
    position = jnp.arange(slot_keys.shape[-1], dtype=jnp.int32)
    in_range = position[None, None, None, :] < valid_rows[:, None, None, None]
    scores = jnp.where(in_range, scores, NEGATIVE_FILL)
    maxima = jnp.max(scores, axis=-1)
    softmax_terms = jnp.where(in_range, jnp.exp(scores - maxima[..., None]), 0.0)
    totals = jnp.sum(softmax_terms, axis=-1)
    weighted = jnp.einsum(
        "nqhp,nhsp->nqhs",
        softmax_terms.astype(jnp.bfloat16),
        slot_values,
        preferred_element_type=jnp.float32,
    )
    return (maxima, totals, weighted)


def combine_blocks(maxima, totals, weighted, onehot):
    owned = onehot.astype(jnp.float32)
    is_live = jnp.sum(owned, axis=1) > 0.5
    masked_max = jnp.where(onehot[:, :, None, None], maxima[:, None, :, :], NEGATIVE_FILL)
    request_max = jnp.max(masked_max, axis=0)
    owner_max = jnp.einsum("nr,rqh->nqh", owned, request_max, precision=lax.Precision.HIGHEST)
    factor = jnp.exp(jnp.where(is_live[:, None, None], maxima - owner_max, NEGATIVE_FILL))
    denominator = jnp.einsum("nr,nqh->rqh", owned, factor * totals, precision=lax.Precision.HIGHEST)
    numerator = jnp.einsum(
        "nr,nqhs->rqhs", owned, factor[..., None] * weighted, precision=lax.Precision.HIGHEST
    )
    return (numerator / denominator[..., None]).astype(jnp.bfloat16)


def layer_norm(summand):
    average = jnp.mean(summand, axis=-1, keepdims=True)
    centred = summand - average
    variance = jnp.mean(centred * centred, axis=-1, keepdims=True)
    return centred * lax.rsqrt(variance + EPSILON)


def local(hist_len, queries, history_keys, cached_history_values, gain_mix, w_up, w_down, gain_out):
    group_size = lax.axis_size(("batch", "hidden"))
    my_index = lax.axis_index(("batch", "hidden"))
    head_size = MODEL_WIDTH // TOKEN_COUNT
    local_heads = history_keys.shape[1] // head_size
    slot_count = history_keys.shape[0]
    score_scale = head_size ** (-0.5)
    query_heads = queries.reshape(TOKEN_COUNT, local_heads, head_size)
    all_lengths = hist_len.reshape(group_size, REQ_DEV)
    peer_ids = jnp.arange(group_size, dtype=jnp.int32)
    mine_hot = peer_ids == my_index
    own_lengths = jnp.sum(jnp.where(mine_hot[:, None], all_lengths, 0), axis=0)
    onehot, valid_rows = slot_layout(own_lengths, slot_count, BLOCK_POSITIONS)
    slot_keys = history_keys.reshape(slot_count, local_heads, head_size, BLOCK_POSITIONS)
    slot_values = cached_history_values.reshape(slot_count, local_heads, head_size, BLOCK_POSITIONS)
    maxima, totals, weighted = block_partials(
        query_heads, slot_keys, slot_values, valid_rows, score_scale
    )
    attended = combine_blocks(maxima, totals, weighted, onehot)
    unmixed = lax.all_to_all(
        attended.reshape(REQ_DEV, TOKEN_COUNT, local_heads * head_size),
        "token",
        split_axis=1,
        concat_axis=2,
        tiled=True,
    )
    mixed_rows = jnp.transpose(attended, (0, 2, 1, 3)).reshape(
        REQ_DEV, local_heads, TOKEN_COUNT * head_size
    )
    joined = mixed_rows.astype(jnp.float32) + unmixed.astype(jnp.float32)
    normed = (layer_norm(joined) * gain_mix).astype(jnp.bfloat16)
    lifted = jnp.einsum(
        "ntd,tdf->ntf",
        lax.all_gather(normed, "hidden", axis=0, tiled=True),
        w_up,
        preferred_element_type=jnp.float32,
    )
    activated = jax.nn.gelu(lifted, approximate=False).astype(jnp.bfloat16)
    partial_sums = jnp.einsum("ntf,tfd->ntd", activated, w_down, preferred_element_type=jnp.float32)
    summed = sent_and_summed(partial_sums.astype(jnp.bfloat16), "hidden", 0)
    return (layer_norm(summed + normed.astype(jnp.float32)) * gain_out).astype(jnp.bfloat16)


def solution(mesh):
    return jax.shard_map(
        local,
        mesh=mesh,
        in_specs=(
            P(),
            P(None, "token"),
            P(("batch", "hidden"), "token", None),
            P(("batch", "hidden"), "token", None),
            P(),
            P("token", None, "hidden"),
            P("token", "hidden", None),
            P(),
        ),
        out_specs=P(("batch", "hidden"), "token", None),
        check_vma=False,
    )
```

profile of v0, /device:TPU:2, one launch (start us, length us, event | category | flops | bytes accessed | tf_op | source)
XLA Modules:
  0.0 88.5 jit_solution(1204152583943687451)
XLA Ops:
  0.0 0.9 reshape.733
  1.1 0.1 reduce.12
  1.6 1.3 %bitcast_reduce_fusion = (f32[96,32]{1,0:T(8,128)S(1)}, f32[1,96,128,32]{2,3,1,0:T(8,128)S(1)}) fusion(bf16[96,48,128]{2,1,0:T(8,128)(2,1)S(1)} %copy-done, bf16[32,48]{1,0:T(8,128)(2,1)} %param.9, pred[96,128]{1,0:T(8,128)(4,1)S(1)} %iota_compare_fusion), kind=kOutput, calls=%fused_computation.4 | convolution fusion | flops 38925312 | bytes 2780160 | tf_op jit(solution)/shard_map/qhs,nhsp->nqhp/dot_general | solution.py:42
  3.0 1.0 %fusion.5 = f32[96,32]{1,0:T(8,128)S(1)} fusion(f32[1,96,128,32]{2,3,1,0:T(8,128)S(1)} %get-tuple-element.10, f32[96,32]{1,0:T(8,128)S(1)} %get-tuple-element.9, pred[96,128]{1,0:T(8,128)(4,1)S(1)} %iota_compare_fusion), kind=kLoop, calls=%fused_computation.11 | loop fusion | flops 1176576 | bytes 1609728 | tf_op jit(solution)/shard_map/reduce_sum | solution.py:50
  4.0 0.2 select_reduce_fusion
  4.3 0.2 fusion.17
  4.6 0.1 fusion.83
  4.7 2.1 %fusion = f32[96,32,48]{2,1,0:T(8,128)S(1)} fusion(bf16[96,48,128]{2,1,0:T(8,128)(2,1)} %param.11, f32[1,96,128,32]{2,3,1,0:T(8,128)S(1)} %get-tuple-element.10, f32[96,32]{1,0:T(8,128)S(1)} %get-tuple-element.9, f32[96,32]{1,0:T(8,128)S(1)} %copy.38, pred[96,128]{1,0:T(8,128)(4,1)S(1)} %iota_compare_fusion), kind=kOutput, calls=%fused_computation.2 | convolution fusion | flops 39075840 | bytes 3379200 | tf_op jit(solution)/shard_map/nqhp,nhsp->nqhs/dot_general | solution.py:51
  6.8 1.6 %fusion.10 = bf16[32,32,48]{2,0,1:T(8,128)(2,1)S(1)} fusion(f32[96,32,48]{2,1,0:T(8,128)S(1)} %fusion, f32[32,32]{0,1:T(8,128)S(1)} %fusion.83, s32[96]{0:T(128)S(1)} %convert_reduce_fusion.2), kind=kOutput, calls=%fused_computation.14 | convolution fusion | flops 56724480 | bytes 692608 | tf_op jit(solution)/shard_map/nr,nqhs->rqhs/dot_general | solution.py:68
  8.4 0.4 reshape.745
  8.7 22.2 %all_to_all.14 = bf16[32,2,768]{2,1,0:T(2,128)(2,1)S(1)} all-to-all(bf16[32,2,768]{2,1,0:T(2,128)(2,1)S(1)} %reshape.745), channel_id=1, replica_groups=mesh['batch'=2,'token'=32,'hidden'=8] {'token'}, dimensions={0} | all-to-all | bytes 196608 | tf_op jit(solution)/shard_map/all_to_all | solution.py:100
  31.0 0.2 reshape.746
  31.2 0.2 fusion.123
  31.5 0.3 copy.42
  31.8 0.3 add.108
  32.0 0.2 multiply_reduce_fusion.1
  32.4 27.8 %all_gather.3 = bf16[256,1,1536]{2,0,1:T(8,128)(2,1)S(1)} all-gather(bf16[32,1,1536]{2,0,1:T(8,128)(2,1)S(1)} %multiply_convert_fusion.2), channel_id=1, replica_groups=mesh['batch'=2,'token'=32,'hidden'=8] {'hidden'}, dimensions={0}, use_global_device_ids=true | all-gather | bytes 884736 | tf_op jit(solution)/shard_map/all_gather | solution.py:114
  60.2 4.4 %convolution_convert_fusion = bf16[256,1536]{1,0:T(8,128)(2,1)} fusion(bf16[1,384,1536]{2,1,0:T(8,128)(2,1)} %param.14, bf16[1,1536,384]{2,1,0:T(8,128)(2,1)} %param.13, bf16[256,1,1536]{2,0,1:T(8,128)(2,1)S(1)} %all_gather.3), kind=kOutput, calls=%fused_computation | convolution fusion | flops 610762752 | bytes 3932160 | tf_op jit(solution)/shard_map/ntf,tfd->ntd/dot_general | solution.py:119
  64.6 5.2 %all-to-all-start.1 = ((bf16[8,32,1,1536]{3,1,2,0:T(8,128)(2,1)}), bf16[8,32,1,1536]{3,1,2,0:T(8,128)(2,1)S(1)}, u32[]{:S(2)}, u32[]{:S(2)}) async-start(bf16[8,32,1,1536]{3,1,2,0:T(8,128)(2,1)} %bitcast.162), calls=%async_computation.1 | async-start | bytes 1572864 | tf_op jit(solution)/shard_map/all_to_all | solution.py:22
  69.9 16.8 %all-to-all-done.1 = bf16[8,32,1,1536]{3,1,2,0:T(8,128)(2,1)S(1)} async-done(((bf16[8,32,1,1536]{3,1,2,0:T(8,128)(2,1)}), bf16[8,32,1,1536]{3,1,2,0:T(8,128)(2,1)S(1)}, u32[]{:S(2)}, u32[]{:S(2)}) %all-to-all-start.1) | async-done | bytes 786464 | tf_op jit(solution)/shard_map/all_to_all | solution.py:22
  86.8 0.2 reduce_sum.113
  87.0 0.5 fusion.24
  87.5 0.2 multiply_reduce_fusion
  87.7 0.8 multiply_convert_fusion.1
  (29 shorter events, 1.1 us)
Async XLA Ops:
  0.0 1.6 %copy-start = (bf16[96,48,128]{2,1,0:T(8,128)(2,1)S(1)}, bf16[96,48,128]{2,1,0:T(8,128)(2,1)}, u32[]{:S(2)}) copy-start(bf16[96,48,128]{2,1,0:T(8,128)(2,1)} %param.10) | copy-start | bytes 3538948
  31.2 1.0 %copy-start.1 = (f32[1536]{0:T(1024)S(1)}, f32[1536]{0:T(1024)}, u32[]{:S(2)}) copy-start(f32[1536]{0:T(1024)} %param.12) | copy-start | bytes 18436
  64.6 22.1 %all-to-all-start.1 = ((bf16[8,32,1,1536]{3,1,2,0:T(8,128)(2,1)}), bf16[8,32,1,1536]{3,1,2,0:T(8,128)(2,1)S(1)}, u32[]{:S(2)}, u32[]{:S(2)}) async-start(bf16[8,32,1,1536]{3,1,2,0:T(8,128)(2,1)} %bitcast.162), calls=%async_computation.1 | async-start | bytes 1572864 | tf_op jit(solution)/shard_map/all_to_all | solution.py:22
  69.9 17.8 %copy-start.2 = (f32[1536]{0:T(1024)S(1)}, f32[1536]{0:T(1024)}, u32[]{:S(2)}) copy-start(f32[1536]{0:T(1024)} %param.15) | copy-start | bytes 18436
where the time goes:
time: 88.8 us; the launch traced here: 88.5 us
  blocking collectives  50.1 us (56%)
  waiting for transfers between devices  16.8 us (19%)
  matrix products  9.73 us (11%)
  starting transfers between devices  5.24 us (6%)
  other arithmetic  3.89 us (4%)
  local copies, waits for them, and re-layouts  2.65 us (3%)
    all_gather x1, blocking collectives, local(): lax.all_gather(normed, 'hidden', axis=0, tiled=True)  27.8 us
    all_to_all x1, blocking collectives, local(): lax.all_to_all(attended.reshape(REQ_DEV, TOKEN_COUNT, local_heads * head_...  22.2 us
    all_to_all x1, waiting for transfers between devices, sent_and_summed(): parts = lax.all_to_all(in_blocks(x, dim, length), axis, 0, 0, tiled=True)  16.8 us
    all_to_all x1, starting transfers between devices, sent_and_summed(): parts = lax.all_to_all(in_blocks(x, dim, length), axis, 0, 0, tiled=True)  5.24 us
    dot_general x1, matrix products, local(): jnp.einsum('ntf,tfd->ntd', activated, w_down, preferred_element_type=jnp....  4.37 us
    dot_general x1, matrix products, block_partials(): jnp.einsum('nqhp,nhsp->nqhs', softmax_terms.astype(jnp.bfloat16), slot_va...  2.12 us
  transfers between devices with their start and end apart: 1, of which 1 were waited for; matrix products, arithmetic and copies ran while one was open for 0% of the time, Pallas kernels for 0%

commit v1 on v0

--- a/solution.py
+++ b/solution.py
@@ -9,6 +9,27 @@
 REQ_DEV = 32
 EPSILON = 1e-05
 NEGATIVE_FILL = -1e30
+
+
+def ring_gather(shard, axis, dim):
+    count, index, width = (lax.axis_size(axis), lax.axis_index(axis), shard.shape[dim])
+    upward = [(i, (i + 1) % count) for i in range(count)]
+    left = [(i, (i - 1) % count) for i in range(count)]
+    whole = jnp.zeros((*shard.shape[:dim], count * width, *shard.shape[dim + 1 :]), shard.dtype)
+    whole = lax.dynamic_update_slice_in_dim(whole, shard, index * width, axis=dim)
+    from_left = from_right = shard
+    half = count // 2
+    for lap in range(1, half + 1):
+        from_left = lax.ppermute(from_left, axis, upward)
+        whole = lax.dynamic_update_slice_in_dim(
+            whole, from_left, (index - lap) % count * width, axis=dim
+        )
+        if lap < count - half:
+            from_right = lax.ppermute(from_right, axis, left)
+            whole = lax.dynamic_update_slice_in_dim(
+                whole, from_right, (index + lap) % count * width, axis=dim
+            )
+    return whole
 
 
 def in_blocks(x, dim, length):
@@ -110,10 +131,7 @@
     joined = mixed_rows.astype(jnp.float32) + unmixed.astype(jnp.float32)
     normed = (layer_norm(joined) * gain_mix).astype(jnp.bfloat16)
     lifted = jnp.einsum(
-        "ntd,tdf->ntf",
-        lax.all_gather(normed, "hidden", axis=0, tiled=True),
-        w_up,
-        preferred_element_type=jnp.float32,
+        "ntd,tdf->ntf", ring_gather(normed, "hidden", 0), w_up, preferred_element_type=jnp.float32
     )
     activated = jax.nn.gelu(lifted, approximate=False).astype(jnp.bfloat16)
     partial_sums = jnp.einsum("ntf,tfd->ntd", activated, w_down, preferred_element_type=jnp.float32)

time: 88.8 us -> 95.4 us (1.074)
  blocking collectives: 50.1 us -> 0 us
  starting transfers between devices: 5.24 us -> 43.6 us
  waiting for transfers between devices: 16.8 us -> 33.5 us
  local copies, waits for them, and re-layouts: 2.65 us -> 3.7 us
    all_gather x1 -> x0, blocking collectives: 27.8 us -> none  [local(): lax.all_gather(normed, 'hidden', axis=0, tiled=True)]
    ppermute x0 -> x7, starting transfers between devices: none -> 23.3 us  [the longest x3 14 us: ring_gather(): from_right = lax.ppermute(from_right, axis, left)]
    all_to_all x1 -> x0, blocking collectives: 22.2 us -> none  [local(): lax.all_to_all(attended.reshape(REQ_DEV, TOKEN_COUNT, local_heads * head_...]
    all_to_all x0 -> x1, starting transfers between devices: none -> 13.5 us  [local(): lax.all_to_all(attended.reshape(REQ_DEV, TOKEN_COUNT, local_heads * head_...]
    all_to_all x0 -> x1, waiting for transfers between devices: none -> 8.84 us  [local(): lax.all_to_all(attended.reshape(REQ_DEV, TOKEN_COUNT, local_heads * head_...]
    ppermute x0 -> x7, waiting for transfers between devices: none -> 7.43 us  [the longest x4 7.42 us: ring_gather(): from_left = lax.ppermute(from_left, axis, upward)]
    all_to_all x1, starting transfers between devices: 5.24 us -> 6.85 us  [sent_and_summed(): parts = lax.all_to_all(in_blocks(x, dim, length), axis, 0, 0, tiled=True)]
  transfers between devices with their start and end apart: 1 -> 9, of which waited for: 1 -> 6; matrix products, arithmetic and copies ran while one was open for 0% -> 0% of each run, Pallas kernels for 0% -> 0%
where the time goes in v1:
time: 95.4 us; the launch traced here: 94.9 us
  starting transfers between devices  43.6 us (46%)
  waiting for transfers between devices  33.5 us (35%)
  matrix products  9.71 us (10%)
  other arithmetic  3.98 us (4%)
  local copies, waits for them, and re-layouts  3.7 us (4%)
    all_to_all x1, waiting for transfers between devices, sent_and_summed(): parts = lax.all_to_all(in_blocks(x, dim, length), axis, 0, 0, tiled=True)  17.2 us
    ppermute x3, starting transfers between devices, ring_gather(): from_right = lax.ppermute(from_right, axis, left)  14 us
    all_to_all x1, starting transfers between devices, local(): lax.all_to_all(attended.reshape(REQ_DEV, TOKEN_COUNT, local_heads * head_...  13.5 us
    ppermute x4, starting transfers between devices, ring_gather(): from_left = lax.ppermute(from_left, axis, upward)  9.32 us
    all_to_all x1, waiting for transfers between devices, local(): lax.all_to_all(attended.reshape(REQ_DEV, TOKEN_COUNT, local_heads * head_...  8.84 us
    ppermute x4, waiting for transfers between devices, ring_gather(): from_left = lax.ppermute(from_left, axis, upward)  7.42 us
    all_to_all x1, starting transfers between devices, sent_and_summed(): parts = lax.all_to_all(in_blocks(x, dim, length), axis, 0, 0, tiled=True)  6.85 us
    dot_general x1, matrix products, local(): jnp.einsum('ntf,tfd->ntd', activated, w_down, preferred_element_type=jnp....  4.37 us
  transfers between devices with their start and end apart: 9, of which 6 were waited for; matrix products, arithmetic and copies ran while one was open for 0% of the time, Pallas kernels for 0%

profile of v1, /device:TPU:2, one launch (start us, length us, event | category | flops | bytes accessed | tf_op | source)
XLA Modules:
  0.0 94.9 jit_solution(12374574574263334846)
XLA Ops:
  0.0 0.9 reshape.775
  1.6 1.3 %bitcast_reduce_fusion = (f32[96,32]{1,0:T(8,128)S(1)}, f32[1,96,128,32]{2,3,1,0:T(8,128)S(1)}) fusion(bf16[96,48,128]{2,1,0:T(8,128)(2,1)S(1)} %copy-done, bf16[32,48]{1,0:T(8,128)(2,1)} %param.9, pred[96,128]{1,0:T(8,128)(4,1)S(1)} %iota_compare_fusion), kind=kOutput, calls=%fused_computation.4 | convolution fusion | flops 38925312 | bytes 2780160 | tf_op jit(solution)/shard_map/qhs,nhsp->nqhp/dot_general | solution.py:63
  3.0 1.0 %fusion.5 = f32[96,32]{1,0:T(8,128)S(1)} fusion(f32[1,96,128,32]{2,3,1,0:T(8,128)S(1)} %get-tuple-element.10, f32[96,32]{1,0:T(8,128)S(1)} %get-tuple-element.9, pred[96,128]{1,0:T(8,128)(4,1)S(1)} %iota_compare_fusion), kind=kLoop, calls=%fused_computation.11 | loop fusion | flops 1176576 | bytes 1609728 | tf_op jit(solution)/shard_map/reduce_sum | solution.py:71
  4.7 2.1 %fusion = f32[96,32,48]{2,1,0:T(8,128)S(1)} fusion(bf16[96,48,128]{2,1,0:T(8,128)(2,1)} %param.11, f32[1,96,128,32]{2,3,1,0:T(8,128)S(1)} %get-tuple-element.10, f32[96,32]{1,0:T(8,128)S(1)} %get-tuple-element.9, f32[96,32]{1,0:T(8,128)S(1)} %copy.40, pred[96,128]{1,0:T(8,128)(4,1)S(1)} %iota_compare_fusion), kind=kOutput, calls=%fused_computation.2 | convolution fusion | flops 39075840 | bytes 3379200 | tf_op jit(solution)/shard_map/nqhp,nhsp->nqhs/dot_general | solution.py:72
  6.8 1.6 %fusion.10 = bf16[32,32,48]{2,0,1:T(8,128)(2,1)S(1)} fusion(f32[96,32,48]{2,1,0:T(8,128)S(1)} %fusion, f32[32,32]{0,1:T(8,128)S(1)} %fusion.77, s32[96]{0:T(128)S(1)} %convert_reduce_fusion.2), kind=kOutput, calls=%fused_computation.14 | convolution fusion | flops 56724480 | bytes 692608 | tf_op jit(solution)/shard_map/nr,nqhs->rqhs/dot_general | solution.py:89
  8.4 1.0 %reshape.793 = bf16[32,2,768]{2,1,0:T(2,128)(2,1)} reshape(bf16[32,32,48]{2,1,0:T(8,128)(2,1)S(1)} %bitcast.167) | data formatting | bytes 196608
  9.4 13.5 %all-to-all-start = ((bf16[32,2,768]{2,1,0:T(2,128)(2,1)}), bf16[32,2,768]{2,1,0:T(2,128)(2,1)S(1)}, u32[]{:S(2)}, u32[]{:S(2)}) async-start(bf16[32,2,768]{2,1,0:T(2,128)(2,1)} %reshape.793), calls=%async_computation | async-start | bytes 196608 | tf_op jit(solution)/shard_map/all_to_all | solution.py:121
  23.0 8.8 %all-to-all-done = bf16[32,2,768]{2,1,0:T(2,128)(2,1)S(1)} async-done(((bf16[32,2,768]{2,1,0:T(2,128)(2,1)}), bf16[32,2,768]{2,1,0:T(2,128)(2,1)S(1)}, u32[]{:S(2)}, u32[]{:S(2)}) %all-to-all-start) | async-done | bytes 98336 | tf_op jit(solution)/shard_map/all_to_all | solution.py:121
  33.4 3.5 %collective-permute-start = (bf16[32,1,1536]{2,0,1:T(8,128)(2,1)S(1)}, bf16[32,1,1536]{2,0,1:T(8,128)(2,1)S(1)}, u32[]{:S(2)}, u32[]{:S(2)}) collective-permute-start(bf16[32,1,1536]{2,0,1:T(8,128)(2,1)S(1)} %multiply_convert_fusion.2), channel_id=1, source_target_pairs={{0,1},{1,2},{2,3},{3,4},{4,5},{5,6},{6,7},{7,0},{8,9},{9,10},{10,1... | collective-permute-start | bytes 294920 | tf_op jit(solution)/shard_map/ppermute | solution.py:23
  36.9 3.8 %collective-permute-start.1 = (bf16[32,1,1536]{2,0,1:T(8,128)(2,1)S(1)}, bf16[32,1,1536]{2,0,1:T(8,128)(2,1)S(1)}, u32[]{:S(2)}, u32[]{:S(2)}) collective-permute-start(bf16[32,1,1536]{2,0,1:T(8,128)(2,1)S(1)} %multiply_convert_fusion.2), channel_id=1, source_target_pairs={{0,7},{1,0},{2,1},{3,2},{4,3},{5,4},{6,5},{7,6},{8,15},{9,8},{10,9... | collective-permute-start | bytes 294920 | tf_op jit(solution)/shard_map/ppermute | solution.py:28
  40.9 0.5 collective-permute-done
  41.4 2.0 %collective-permute-start.2 = (bf16[32,1,1536]{2,0,1:T(8,128)(2,1)S(1)}, bf16[32,1,1536]{2,0,1:T(8,128)(2,1)S(1)}, u32[]{:S(2)}, u32[]{:S(2)}) collective-permute-start(bf16[32,1,1536]{2,0,1:T(8,128)(2,1)S(1)} %collective-permute-done), channel_id=1, source_target_pairs={{0,1},{1,2},{2,3},{3,4},{4,5},{5,6},{6,7},{7,0},{8,9},{9,10},{10,1... | collective-permute-start | bytes 294920 | tf_op jit(solution)/shard_map/ppermute | solution.py:23
  43.4 5.0 %collective-permute-start.3 = (bf16[32,1,1536]{2,0,1:T(8,128)(2,1)S(1)}, bf16[32,1,1536]{2,0,1:T(8,128)(2,1)S(1)}, u32[]{:S(2)}, u32[]{:S(2)}) collective-permute-start(bf16[32,1,1536]{2,0,1:T(8,128)(2,1)S(1)} %collective-permute-done.1), channel_id=1, source_target_pairs={{0,7},{1,0},{2,1},{3,2},{4,3},{5,4},{6,5},{7,6},{8,15},{9,8},{10,9... | collective-permute-start | bytes 294920 | tf_op jit(solution)/shard_map/ppermute | solution.py:28
  48.5 0.6 collective-permute-done.2
  49.1 1.9 %collective-permute-start.4 = (bf16[32,1,1536]{2,0,1:T(8,128)(2,1)S(1)}, bf16[32,1,1536]{2,0,1:T(8,128)(2,1)S(1)}, u32[]{:S(2)}, u32[]{:S(2)}) collective-permute-start(bf16[32,1,1536]{2,0,1:T(8,128)(2,1)S(1)} %collective-permute-done.2), channel_id=1, source_target_pairs={{0,1},{1,2},{2,3},{3,4},{4,5},{5,6},{6,7},{7,0},{8,9},{9,10},{10,1... | collective-permute-start | bytes 294920 | tf_op jit(solution)/shard_map/ppermute | solution.py:23
  51.1 5.1 %collective-permute-start.5 = (bf16[32,1,1536]{2,0,1:T(8,128)(2,1)S(1)}, bf16[32,1,1536]{2,0,1:T(8,128)(2,1)S(1)}, u32[]{:S(2)}, u32[]{:S(2)}) collective-permute-start(bf16[32,1,1536]{2,0,1:T(8,128)(2,1)S(1)} %collective-permute-done.3), channel_id=1, source_target_pairs={{0,7},{1,0},{2,1},{3,2},{4,3},{5,4},{6,5},{7,6},{8,15},{9,8},{10,9... | collective-permute-start | bytes 294920 | tf_op jit(solution)/shard_map/ppermute | solution.py:28
  56.2 0.6 collective-permute-done.4
  56.8 1.9 %collective-permute-start.6 = (bf16[32,1,1536]{2,0,1:T(8,128)(2,1)S(1)}, bf16[32,1,1536]{2,0,1:T(8,128)(2,1)S(1)}, u32[]{:S(2)}, u32[]{:S(2)}) collective-permute-start(bf16[32,1,1536]{2,0,1:T(8,128)(2,1)S(1)} %collective-permute-done.4), channel_id=1, source_target_pairs={{0,1},{1,2},{2,3},{3,4},{4,5},{5,6},{6,7},{7,0},{8,9},{9,10},{10,1... | collective-permute-start | bytes 294920 | tf_op jit(solution)/shard_map/ppermute | solution.py:23
  58.8 5.7 %collective-permute-done.6 = bf16[32,1,1536]{2,0,1:T(8,128)(2,1)S(1)} collective-permute-done((bf16[32,1,1536]{2,0,1:T(8,128)(2,1)S(1)}, bf16[32,1,1536]{2,0,1:T(8,128)(2,1)S(1)}, u32[]{:S(2)}, u32[]{:S(2)}) %collective-permute-start.6) | collective-permute-done | bytes 98336 | tf_op jit(solution)/shard_map/ppermute | solution.py:23
  64.6 4.4 %convolution_convert_fusion = bf16[256,1536]{1,0:T(8,128)(2,1)} fusion(bf16[1,384,1536]{2,1,0:T(8,128)(2,1)} %param.14, bf16[256,1536]{1,0:T(8,128)(2,1)S(1)} %bitcast_dynamic-update-slice_fusion, bf16[1,1536,384]{2,1,0:T(8,128)(2,1)} %param.13), kind=kOutput, calls=%fused_computation | convolution fusion | flops 610762752 | bytes 3932160 | tf_op jit(solution)/shard_map/ntf,tfd->ntd/dot_general | solution.py:137
  68.9 6.8 %all-to-all-start.1 = ((bf16[8,32,1,1536]{3,1,2,0:T(8,128)(2,1)}), bf16[8,32,1,1536]{3,1,2,0:T(8,128)(2,1)S(1)}, u32[]{:S(2)}, u32[]{:S(2)}) async-start(bf16[8,32,1,1536]{3,1,2,0:T(8,128)(2,1)} %bitcast.168), calls=%async_computation.1 | async-start | bytes 1572864 | tf_op jit(solution)/shard_map/all_to_all | solution.py:43
  75.9 17.2 %all-to-all-done.1 = bf16[8,32,1,1536]{3,1,2,0:T(8,128)(2,1)S(1)} async-done(((bf16[8,32,1,1536]{3,1,2,0:T(8,128)(2,1)}), bf16[8,32,1,1536]{3,1,2,0:T(8,128)(2,1)S(1)}, u32[]{:S(2)}, u32[]{:S(2)}) %all-to-all-start.1) | async-done | bytes 786464 | tf_op jit(solution)/shard_map/all_to_all | solution.py:43
  93.4 0.5 fusion.23
  94.2 0.8 multiply_convert_fusion.1
  (53 shorter events, 4.0 us)
Async XLA Ops:
  0.0 1.6 %copy-start = (bf16[96,48,128]{2,1,0:T(8,128)(2,1)S(1)}, bf16[96,48,128]{2,1,0:T(8,128)(2,1)}, u32[]{:S(2)}) copy-start(bf16[96,48,128]{2,1,0:T(8,128)(2,1)} %param.10) | copy-start | bytes 3538948
  9.4 22.4 %all-to-all-start = ((bf16[32,2,768]{2,1,0:T(2,128)(2,1)}), bf16[32,2,768]{2,1,0:T(2,128)(2,1)S(1)}, u32[]{:S(2)}, u32[]{:S(2)}) async-start(bf16[32,2,768]{2,1,0:T(2,128)(2,1)} %reshape.793), calls=%async_computation | async-start | bytes 196608 | tf_op jit(solution)/shard_map/all_to_all | solution.py:121
  32.3 1.1 %copy-start.1 = (f32[1536]{0:T(1024)S(1)}, f32[1536]{0:T(1024)}, u32[]{:S(2)}) copy-start(f32[1536]{0:T(1024)} %param.12) | copy-start | bytes 18436
  33.4 8.0 %collective-permute-start = (bf16[32,1,1536]{2,0,1:T(8,128)(2,1)S(1)}, bf16[32,1,1536]{2,0,1:T(8,128)(2,1)S(1)}, u32[]{:S(2)}, u32[]{:S(2)}) collective-permute-start(bf16[32,1,1536]{2,0,1:T(8,128)(2,1)S(1)} %multiply_convert_fusion.2), channel_id=1, source_target_pairs={{0,1},{1,2},{2,3},{3,4},{4,5},{5,6},{6,7},{7,0},{8,9},{9,10},{10,1... | collective-permute-start | bytes 294920 | tf_op jit(solution)/shard_map/ppermute | solution.py:23
  36.9 6.5 %collective-permute-start.1 = (bf16[32,1,1536]{2,0,1:T(8,128)(2,1)S(1)}, bf16[32,1,1536]{2,0,1:T(8,128)(2,1)S(1)}, u32[]{:S(2)}, u32[]{:S(2)}) collective-permute-start(bf16[32,1,1536]{2,0,1:T(8,128)(2,1)S(1)} %multiply_convert_fusion.2), channel_id=1, source_target_pairs={{0,7},{1,0},{2,1},{3,2},{4,3},{5,4},{6,5},{7,6},{8,15},{9,8},{10,9... | collective-permute-start | bytes 294920 | tf_op jit(solution)/shard_map/ppermute | solution.py:28
  41.4 7.7 %collective-permute-start.2 = (bf16[32,1,1536]{2,0,1:T(8,128)(2,1)S(1)}, bf16[32,1,1536]{2,0,1:T(8,128)(2,1)S(1)}, u32[]{:S(2)}, u32[]{:S(2)}) collective-permute-start(bf16[32,1,1536]{2,0,1:T(8,128)(2,1)S(1)} %collective-permute-done), channel_id=1, source_target_pairs={{0,1},{1,2},{2,3},{3,4},{4,5},{5,6},{6,7},{7,0},{8,9},{9,10},{10,1... | collective-permute-start | bytes 294920 | tf_op jit(solution)/shard_map/ppermute | solution.py:23
  43.4 7.6 %collective-permute-start.3 = (bf16[32,1,1536]{2,0,1:T(8,128)(2,1)S(1)}, bf16[32,1,1536]{2,0,1:T(8,128)(2,1)S(1)}, u32[]{:S(2)}, u32[]{:S(2)}) collective-permute-start(bf16[32,1,1536]{2,0,1:T(8,128)(2,1)S(1)} %collective-permute-done.1), channel_id=1, source_target_pairs={{0,7},{1,0},{2,1},{3,2},{4,3},{5,4},{6,5},{7,6},{8,15},{9,8},{10,9... | collective-permute-start | bytes 294920 | tf_op jit(solution)/shard_map/ppermute | solution.py:28
  49.1 7.7 %collective-permute-start.4 = (bf16[32,1,1536]{2,0,1:T(8,128)(2,1)S(1)}, bf16[32,1,1536]{2,0,1:T(8,128)(2,1)S(1)}, u32[]{:S(2)}, u32[]{:S(2)}) collective-permute-start(bf16[32,1,1536]{2,0,1:T(8,128)(2,1)S(1)} %collective-permute-done.2), channel_id=1, source_target_pairs={{0,1},{1,2},{2,3},{3,4},{4,5},{5,6},{6,7},{7,0},{8,9},{9,10},{10,1... | collective-permute-start | bytes 294920 | tf_op jit(solution)/shard_map/ppermute | solution.py:23
  51.1 7.7 %collective-permute-start.5 = (bf16[32,1,1536]{2,0,1:T(8,128)(2,1)S(1)}, bf16[32,1,1536]{2,0,1:T(8,128)(2,1)S(1)}, u32[]{:S(2)}, u32[]{:S(2)}) collective-permute-start(bf16[32,1,1536]{2,0,1:T(8,128)(2,1)S(1)} %collective-permute-done.3), channel_id=1, source_target_pairs={{0,7},{1,0},{2,1},{3,2},{4,3},{5,4},{6,5},{7,6},{8,15},{9,8},{10,9... | collective-permute-start | bytes 294920 | tf_op jit(solution)/shard_map/ppermute | solution.py:28
  56.8 7.7 %collective-permute-start.6 = (bf16[32,1,1536]{2,0,1:T(8,128)(2,1)S(1)}, bf16[32,1,1536]{2,0,1:T(8,128)(2,1)S(1)}, u32[]{:S(2)}, u32[]{:S(2)}) collective-permute-start(bf16[32,1,1536]{2,0,1:T(8,128)(2,1)S(1)} %collective-permute-done.4), channel_id=1, source_target_pairs={{0,1},{1,2},{2,3},{3,4},{4,5},{5,6},{6,7},{7,0},{8,9},{9,10},{10,1... | collective-permute-start | bytes 294920 | tf_op jit(solution)/shard_map/ppermute | solution.py:23
  68.9 24.2 %all-to-all-start.1 = ((bf16[8,32,1,1536]{3,1,2,0:T(8,128)(2,1)}), bf16[8,32,1,1536]{3,1,2,0:T(8,128)(2,1)S(1)}, u32[]{:S(2)}, u32[]{:S(2)}) async-start(bf16[8,32,1,1536]{3,1,2,0:T(8,128)(2,1)} %bitcast.168), calls=%async_computation.1 | async-start | bytes 1572864 | tf_op jit(solution)/shard_map/all_to_all | solution.py:43
  75.9 18.3 %copy-start.2 = (f32[1536]{0:T(1024)S(1)}, f32[1536]{0:T(1024)}, u32[]{:S(2)}) copy-start(f32[1536]{0:T(1024)} %param.15) | copy-start | bytes 18436
